TPU v7x, 32 devices: a whole 2x2x4 slice. The times are simulated.
32 devices in a mesh: groups: 2 (over y), cuts: 2 (over x), row: 4 (over z), sub: 2 (over core).
Axes of the slice: x: 2, y: 2, z: 4, core: 2. Of those that a mesh axis runs over, the one named last changes fastest.
Arguments:
- hop: bfloat16 [48, 6, 128, 128], P(('groups', 'row')), parts along dimension 0, may hold values from -0.21875 to 0.21875
- pattern: int32 [48, 6], P(('groups', 'row')), parts along dimension 0, may hold values from 0 to 23, as said below
- vectors: bfloat16 [2, 6144, 512], P('cuts', ('groups', 'row'), 'sub'), parts along dimension 1, may hold values from -6 to 6
- counts: int32 [4], P(('groups', 'cuts')), parts along dimension 0, may hold values from 256 to 512, as said below
- center: float32 [4], P(('groups', 'cuts')), parts along dimension 0, may hold values from -1 to 1
- halfwidth: float32 [4], P(('groups', 'cuts')), parts along dimension 0, may hold values from 1.5 to 3
Outputs:
- margin: float32 [4, 2, 256, 512], P(('groups', 'cuts'), 'sub', 'row'), parts along dimension 0
There are 2 independent parts, one for each index of `groups`. A program takes and returns all parts, laid end to end along the dimension named above; each array names one. Nothing has to cross between parts.
Inputs may be any that keep to these rules, and one draw needn't show every extreme that they name: `pattern`: block row i's stored blocks lie in block columns (i + o) mod 24 for 6 distinct offsets o between -3 and 3; the offsets 0, -3 and 3 appear in every block row. `counts`: at least one slice has all 512 vectors live.
All inputs are finite; a program needn't handle non-finite values.
Results may differ from a plain program's by a relative error of at most 0.00061.
Values may be sent and summed in bfloat16 or wider, within the bound.
No kernel may reach another device: no remote copies, remote signals or barrier semaphores. Data moves between devices by JAX's collectives and lax.ppermute only.
A program may use at most 64 MiB of HBM per device.

v0:
```python
import functools

import jax
import jax.numpy as jnp
from jax import lax
from jax.experimental import pallas as pl
from jax.experimental.pallas import tpu as pltpu
from jax.sharding import PartitionSpec as P

W = 3
LIMIT = 16 * 1024 * 1024
COST = pl.CostEstimate(flops=1000, bytes_accessed=1000, transcendentals=0)
LONG = pl.CostEstimate(flops=20_000_000_000, bytes_accessed=1000, transcendentals=0)
VMEM = pl.BlockSpec(memory_space=pltpu.VMEM)
SMEM = pl.BlockSpec(memory_space=pltpu.SMEM)


def call(kernel, out_shape, in_specs, cost=COST):
    return pl.pallas_call(
        kernel,
        out_shape=out_shape,
        in_specs=in_specs,
        out_specs=jax.tree.map(lambda _: VMEM, out_shape),
        compiler_params=pltpu.CompilerParams(vmem_limit_bytes=LIMIT),
        cost_estimate=cost,
    )


def mm(a, b):
    return jnp.dot(a, b, preferred_element_type=jnp.float32)


def tmm(a, b):
    return lax.dot_general(a, b, (((0,), (0,)), ((), ())), preferred_element_type=jnp.float32)


def after(value, other):
    return lax.optimization_barrier((value, other))[0]


def ids_kernel(out_ref):
    out_ref[...] = lax.broadcasted_iota(jnp.int32, out_ref.shape, 1) + lax.axis_index("sub") * out_ref.shape[1]


def ids_of(half):
    return call(ids_kernel, jax.ShapeDtypeStruct((8, half), jnp.int32), [], LONG)()


def table_kernel(center_ref, width_ref, ids_ref, table_ref):
    line = lax.broadcasted_iota(jnp.int32, table_ref.shape, 0)
    table_ref[...] = jnp.where(line == 0, center_ref[0], width_ref[0])


def table_of(center, halfwidth, ids):
    shape = jax.ShapeDtypeStruct(ids.shape, jnp.float32)
    return call(table_kernel, shape, [SMEM] * 2 + [VMEM])(after(center, ids), after(halfwidth, ids), ids)


def live_kernel(counts_ref, ids_ref, live_ref):
    live_ref[...] = jnp.where(ids_ref[...] < counts_ref[0], 1.0, 0.0)


def live_of(counts, ids):
    return call(live_kernel, jax.ShapeDtypeStruct(ids.shape, jnp.float32), [SMEM, VMEM])(counts, ids)


def band_kernel(total_blocks, table_ref, pattern_ref, hop_ref, xa_ref, xb_ref, band_ref, image_ref):
    rows_dev, stored, block, _ = hop_ref.shape
    wide = W * block
    first_block = lax.axis_index("row") * rows_dev
    band_ref[...] = jnp.zeros_like(band_ref)
    for r in range(rows_dev):
        rows = slice(r * block, (r + 1) * block)
        for k in range(stored):
            col = lax.rem(pattern_ref[r, k] - first_block + (W + total_blocks), total_blocks) - W
            inside = jnp.logical_and(col >= 0, col < rows_dev)
            halo = 2 * W + jnp.where(col < 0, col + W, col - rows_dev)
            at = jnp.where(inside, col, halo)
            band_ref[rows, pl.ds(pl.multiple_of(at * block, block), block)] = hop_ref[r, k]
    image_ref[...] = mm(band_ref[:, :wide], xa_ref[...]) + mm(band_ref[:, wide:2 * wide], xb_ref[...])


def band_parts(table, hop, pattern, xa, xb, total_blocks):
    rows_dev, _, block, _ = hop.shape
    wide, tall, half = W * block, rows_dev * block, xa.shape[1]
    return call(
        functools.partial(band_kernel, total_blocks),
        (
            jax.ShapeDtypeStruct((tall, 3 * wide), hop.dtype),
            jax.ShapeDtypeStruct((tall, half), jnp.float32),
        ),
        [VMEM, SMEM] + [VMEM] * 3,
    )(table, pattern, hop, xa, xb)


def halo_image(side, band_ref, image_ref, halo_ref):
    wide = halo_ref.shape[0]
    rows = slice(side * wide, (side + 1) * wide)
    return image_ref[rows, :] + mm(band_ref[rows, 2 * wide:], halo_ref[...])


def step_kernel(side, table_ref, image_ref, band_ref, halo_ref, x_ref, out_ref):
    shift, width = table_ref[0:1, :], table_ref[1:2, :]
    image = halo_image(side, band_ref, image_ref, halo_ref)
    out_ref[...] = ((image - shift * x_ref[...].astype(jnp.float32)) / width).astype(jnp.bfloat16)


def step(side, table, image, band, halo, x):
    shape = jax.ShapeDtypeStruct(x.shape, jnp.bfloat16)
    return call(functools.partial(step_kernel, side), shape, [VMEM] * 5)(table, image, band, halo, x)


def finish_kernel(side, table_ref, live_ref, image_ref, band_ref, halo_ref, s_ref, x_ref, out_ref):
    shift, width = table_ref[0:1, :], table_ref[1:2, :]
    live = live_ref[0:1, :] > 0.0
    image = halo_image(side, band_ref, image_ref, halo_ref)
    value = 2.0 * (image - shift * s_ref[...].astype(jnp.float32)) / width - x_ref[...].astype(jnp.float32)
    out_ref[...] = jnp.where(live, value, 0.0).astype(jnp.bfloat16)


def finish(side, table, live, image, band, halo, s, x):
    shape = jax.ShapeDtypeStruct(x.shape, jnp.bfloat16)
    return call(functools.partial(finish_kernel, side), shape, [VMEM] * 7)(table, live, image, band, halo, s, x)


def exponent(value):
    top = jnp.max(jnp.abs(value), axis=(0, 1), keepdims=True)
    return jnp.clip(jnp.ceil(jnp.log2(jnp.maximum(top, 1e-36))) - 14.0, -100.0, 60.0)


def with_code(share, line, same, e):
    row = lax.broadcasted_iota(jnp.int32, same.shape, 0)
    col = lax.broadcasted_iota(jnp.int32, same.shape, 1)
    return jnp.where((lax.rem(row, share) == line) & (col == row - line), e, same)


def early_kernel(share, fa_ref, fb_ref, oa_ref, out_ref):
    half = fa_ref.shape[1]
    fa, fb = fa_ref[...], fb_ref[...]
    same = tmm(fa, fa) + tmm(fb, fb)
    e = exponent(same)
    out_ref[:, :half] = with_code(share, 1, same * jnp.exp2(-e), e)
    out_ref[:, half:] = tmm(fa, oa_ref[...])


def early_terms(fa, fb, oa, share):
    half = fa.shape[1]
    shape = jax.ShapeDtypeStruct((half, 2 * half), jnp.float32)
    return call(functools.partial(early_kernel, share), shape, [VMEM] * 3)(fa, fb, oa)


def code_kernel(share, early_ref, fb_ref, ob_ref, out_ref):
    half = fb_ref.shape[1]
    cross = early_ref[:, half:] + tmm(fb_ref[...], ob_ref[...])
    e = exponent(cross)
    out_ref[:, :half] = with_code(share, 2, early_ref[:, :half], e)
    out_ref[:, half:] = cross * jnp.exp2(-e)


def code_terms(early, fb, ob, share):
    shape = jax.ShapeDtypeStruct(early.shape, jnp.float32)
    return call(functools.partial(code_kernel, share), shape, [VMEM] * 3)(early, fb, ob)


def pick(head, shift, share):
    col = lax.broadcasted_iota(jnp.int32, head.shape, 1)
    here = col == lax.axis_index("row") * share + shift
    return jnp.sum(jnp.where(here, head, 0.0), axis=1, keepdims=True)


def factors(head, share, order_total):
    scale = jnp.exp2(pick(head, 0, share)) / order_total
    return scale[1:2], scale[2:3]


def first_sum_kernel(order_total, coded_ref, piece_ref, out_ref):
    share, half = out_ref.shape[0], out_ref.shape[1] // 2
    mine = coded_ref.at[pl.ds(pl.multiple_of(lax.axis_index("row") * share, 8), share), :]
    own_same, own_cross = factors(mine[:8, :half], share, order_total)
    same, cross = factors(piece_ref[:8, :half], share, order_total)
    out_ref[:, :half] = mine[:, :half] * own_same + piece_ref[:, :half] * same
    out_ref[:, half:] = mine[:, half:] * own_cross + piece_ref[:, half:] * cross


def first_sum(coded, piece, order_total):
    shape = jax.ShapeDtypeStruct(piece.shape, jnp.float32)
    return call(functools.partial(first_sum_kernel, order_total), shape, [VMEM] * 2, LONG)(coded, piece)


def add_kernel(order_total, sum_ref, piece_ref, out_ref):
    share, half = out_ref.shape[0], out_ref.shape[1] // 2
    same, cross = factors(piece_ref[:8, :half], share, order_total)
    out_ref[:, :half] = sum_ref[:, :half] + piece_ref[:, :half] * same
    out_ref[:, half:] = sum_ref[:, half:] + piece_ref[:, half:] * cross


def add_piece(total, piece, order_total):
    shape = jax.ShapeDtypeStruct(total.shape, jnp.float32)
    return call(functools.partial(add_kernel, order_total), shape, [VMEM] * 2, LONG)(total, piece)


def last_kernel(order_total, sum_ref, piece_ref, out_ref):
    share, half = out_ref.shape[0], out_ref.shape[1] // 2
    same, cross = factors(piece_ref[:8, :half], share, order_total)
    sub = lax.axis_index("sub")
    at = pl.ds(pl.multiple_of(sub * half, half), half)
    other = pl.ds(pl.multiple_of((1 - sub) * half, half), half)
    out_ref[:, other] = sum_ref[:, half:] + piece_ref[:, half:] * cross
    out_ref[:, at] = sum_ref[:, :half] + piece_ref[:, :half] * same
    head = sum_ref[:8, :half] + piece_ref[:8, :half] * same
    row = lax.broadcasted_iota(jnp.int32, head.shape, 0)
    col = lax.broadcasted_iota(jnp.int32, head.shape, 1)
    start = col == lax.axis_index("row") * share
    for line in (1, 2):
        head = jnp.where((row == line) & start, pick(head[:1], line, share), head)
    out_ref[:8, at] = head


def last_sum(total, piece, order_total):
    shape = jax.ShapeDtypeStruct(total.shape, jnp.float32)
    return call(functools.partial(last_kernel, order_total), shape, [VMEM] * 2)(total, piece)


def image_kernel(band_ref, sa_ref, sb_ref, out_ref):
    wide = sa_ref.shape[0]
    out_ref[...] = mm(band_ref[:, :wide], sa_ref[...]) + mm(band_ref[:, wide:2 * wide], sb_ref[...])


def own_image(band, sa, sb):
    shape = jax.ShapeDtypeStruct((band.shape[0], sa.shape[1]), jnp.float32)
    return call(image_kernel, shape, [VMEM] * 3)(band, sa, sb)


def send_shares(coded, row_count, share):
    me = lax.axis_index("row")
    arrived = []
    for shift in range(1, row_count):
        part = lax.dynamic_slice_in_dim(coded, (me + shift) % row_count * share, share, axis=0)
        ring = [(i, (i + shift) % row_count) for i in range(row_count)]
        arrived.append(lax.ppermute(part, "row", ring))
    return arrived


def body(hop, pattern, vectors, counts, center, halfwidth):
    rows_dev = hop.shape[0]
    block = hop.shape[2]
    half = vectors.shape[2]
    row_count = lax.axis_size("row")
    total_blocks = rows_dev * row_count
    order_total = total_blocks * block
    wide = W * block
    share = half // row_count
    assert rows_dev == 2 * W
    forward = [(i, (i + 1) % row_count) for i in range(row_count)]
    backward = [(target, source) for source, target in forward]
    swap = [(0, 1), (1, 0)]

    def halos_of(low, high):
        return lax.ppermute(high, "row", forward), lax.ppermute(low, "row", backward)

    x = vectors[0]
    xa, xb = x[:wide], x[wide:]
    halo_a, halo_b = halos_of(xa, xb)
    ids = ids_of(half)
    table = table_of(center, halfwidth, ids)
    band, image = band_parts(table, hop, pattern, xa, xb, total_blocks)
    sb = step(1, table, image, band, halo_b, xb)
    sa = step(0, table, image, band, lax.optimization_barrier((halo_a, sb))[0], xa)
    halo_a, halo_b = halos_of(sa, sb)
    image = own_image(band, sa, sb)
    live = live_of(after(counts, sa), ids)
    fa = finish(0, table, live, image, band, halo_a, sa, xa)
    oa = lax.ppermute(fa, "sub", swap)
    fb = finish(1, table, live, image, band, lax.optimization_barrier((halo_b, fa))[0], sb, xb)
    ob = lax.ppermute(fb, "sub", swap)
    coded = code_terms(early_terms(fa, fb, oa, share), fb, ob, share)
    first, *middle, last = send_shares(coded.astype(jnp.float16), row_count, share)
    total = first_sum(coded, first.astype(jnp.float32), order_total)
    for piece in middle:
        total = add_piece(total, piece.astype(jnp.float32), order_total)
    total, last = lax.optimization_barrier((total, last))
    margin = last_sum(total, last.astype(jnp.float32), order_total)
    return margin.reshape(1, 1, share, 2 * half)


def solution(mesh):
    in_specs = (
        P(("groups", "row"), None, None, None),
        P(("groups", "row"), None),
        P("cuts", ("groups", "row"), "sub"),
        P(("groups", "cuts")),
        P(("groups", "cuts")),
        P(("groups", "cuts")),
    )
    out_specs = P(("groups", "cuts"), "sub", "row", None)
    return jax.shard_map(body, mesh=mesh, in_specs=in_specs, out_specs=out_specs, check_vma=False)
```

profile of v0, /device:TPU:0, one launch (start us, length us, event | category | flops | bytes accessed | tf_op | source)
XLA Modules:
  0.0 36.4 jit_solution(18432268389286295088)
XLA Ops:
  0.0 1.0 %slice_bitcast_fusion = (bf16[384,256]{1,0:T(8,128)(2,1)S(1)}, bf16[384,256]{1,0:T(8,128)(2,1)S(1)}) fusion(bf16[1,768,256]{2,1,0:T(8,128)(2,1)} %param.8), kind=kLoop, calls=%fused_computation | loop fusion | bytes 786432 | tf_op jit(solution)/shard_map/slice | solution.py:262
  1.1 5.1 %collective-permute-start.1 = (bf16[384,256]{1,0:T(8,128)(2,1)S(1)}, bf16[384,256]{1,0:T(8,128)(2,1)S(1)}, u32[]{:S(2)}, u32[]{:S(2)}) collective-permute-start(bf16[384,256]{1,0:T(8,128)(2,1)S(1)} %get-tuple-element.24.xa_ref.x_ref), channel_id=1, source_target_pairs={{2,0},{4,2},{6,4},{0,6},{3,1},{5,3},{7,5},{1,7},{10,8},{12,10},{14... | collective-permute-start | bytes 589832 | tf_op jit(solution)/shard_map/ppermute | solution.py:259
  6.2 0.0 copy-start
  6.2 0.0 copy-start.1
  6.2 0.0 collective-permute-start
  7.6 0.0 copy-done
  7.6 0.0 copy-done.1
  7.6 1.5 %shard_map.66 = (bf16[768,1152]{1,0:T(8,128)(2,1)S(1)}, f32[768,256]{1,0:T(8,128)S(1)}) custom-call(f32[8,256]{1,0:T(8,128)S(1)} %shard_map.65.table_ref, s32[6,6]{1,0:T(8,128)S(1)} %copy-done.1, bf16[6,6,128,128]{3,2,1,0:T(8,128)(2,1)S(1)} %copy-done, bf16[384,256]{1,0:T(8,128)(2,1)S(1)} %get-tuple-element.24.xa_ref.x_ref, ...), custom_call_target="tpu_custom_call" | custom-call | flops 1000 | bytes 1000 | tf_op jit(solution)/shard_map/pallas_call | solution.py:86
  9.1 2.3 %collective-permute-done.1.halo_ref = bf16[384,256]{1,0:T(8,128)(2,1)S(1)} collective-permute-done((bf16[384,256]{1,0:T(8,128)(2,1)S(1)}, bf16[384,256]{1,0:T(8,128)(2,1)S(1)}, u32[]{:S(2)}, u32[]{:S(2)}) %collective-permute-start.1) | collective-permute-done | bytes 196640 | tf_op jit(solution)/shard_map/ppermute | solution.py:259
  11.5 0.3 shard_map.67.sb_ref.s_ref
  11.7 0.1 collective-permute-start.2
  11.8 4.2 %collective-permute-done.halo_ref = bf16[384,256]{1,0:T(8,128)(2,1)S(1)} collective-permute-done((bf16[384,256]{1,0:T(8,128)(2,1)S(1)}, bf16[384,256]{1,0:T(8,128)(2,1)S(1)}, u32[]{:S(2)}, u32[]{:S(2)}) %collective-permute-start) | collective-permute-done | bytes 196640 | tf_op jit(solution)/shard_map/ppermute | solution.py:259
  16.0 0.3 shard_map.68.sa_ref.s_ref
  16.2 1.8 %collective-permute-start.3 = (bf16[384,256]{1,0:T(8,128)(2,1)S(1)}, bf16[384,256]{1,0:T(8,128)(2,1)S(1)}, u32[]{:S(2)}, u32[]{:S(2)}) collective-permute-start(bf16[384,256]{1,0:T(8,128)(2,1)S(1)} %shard_map.68.sa_ref.s_ref), channel_id=1, source_target_pairs={{2,0},{4,2},{6,4},{0,6},{3,1},{5,3},{7,5},{1,7},{10,8},{12,10},{14... | collective-permute-start | bytes 589832 | tf_op jit(solution)/shard_map/ppermute | solution.py:259
  18.7 0.6 %shard_map.70.image_ref = f32[768,256]{1,0:T(8,128)S(1)} custom-call(bf16[768,1152]{1,0:T(8,128)(2,1)S(1)} %get-tuple-element.17.band_ref, bf16[384,256]{1,0:T(8,128)(2,1)S(1)} %shard_map.68.sa_ref.s_ref, bf16[384,256]{1,0:T(8,128)(2,1)S(1)} %shard_map.67.sb_ref.s_ref), custom_call_target="tpu_custom_call" | custom-call | flops 1000 | bytes 1000 | tf_op jit(solution)/shard_map/pallas_call | solution.py:231
  19.3 2.6 %collective-permute-done.2.halo_ref = bf16[384,256]{1,0:T(8,128)(2,1)S(1)} collective-permute-done((bf16[384,256]{1,0:T(8,128)(2,1)S(1)}, bf16[384,256]{1,0:T(8,128)(2,1)S(1)}, u32[]{:S(2)}, u32[]{:S(2)}) %collective-permute-start.2) | collective-permute-done | bytes 196640 | tf_op jit(solution)/shard_map/ppermute | solution.py:259
  21.9 0.3 shard_map.71.fa_ref
  22.2 0.1 collective-permute-start.4
  22.2 1.6 %collective-permute-done.3.halo_ref = bf16[384,256]{1,0:T(8,128)(2,1)S(1)} collective-permute-done((bf16[384,256]{1,0:T(8,128)(2,1)S(1)}, bf16[384,256]{1,0:T(8,128)(2,1)S(1)}, u32[]{:S(2)}, u32[]{:S(2)}) %collective-permute-start.3) | collective-permute-done | bytes 196640 | tf_op jit(solution)/shard_map/ppermute | solution.py:259
  23.9 0.3 shard_map.72.fb_ref
  24.1 0.1 collective-permute-start.5
  24.3 0.0 collective-permute-done.4.oa_ref
  24.3 0.5 %shard_map.73.early_ref = f32[256,512]{1,0:T(8,128)S(1)} custom-call(bf16[384,256]{1,0:T(8,128)(2,1)S(1)} %shard_map.71.fa_ref, bf16[384,256]{1,0:T(8,128)(2,1)S(1)} %shard_map.72.fb_ref, bf16[384,256]{1,0:T(8,128)(2,1)S(1)} %collective-permute-done.4.oa_ref), custom_call_target="tpu_custom_call" | custom-call | flops 1000 | bytes 1000 | tf_op jit(solution)/shard_map/pallas_call | solution.py:149
  24.8 0.8 %collective-permute-done.5.ob_ref = bf16[384,256]{1,0:T(8,128)(2,1)S(1)} collective-permute-done((bf16[384,256]{1,0:T(8,128)(2,1)S(1)}, bf16[384,256]{1,0:T(8,128)(2,1)S(1)}, u32[]{:S(2)}, u32[]{:S(2)}) %collective-permute-start.5) | collective-permute-done | bytes 196640 | tf_op jit(solution)/shard_map/ppermute | solution.py:275
  25.6 0.4 %shard_map.74.coded_ref = f32[256,512]{1,0:T(8,128)S(1)} custom-call(f32[256,512]{1,0:T(8,128)S(1)} %shard_map.73.early_ref, bf16[384,256]{1,0:T(8,128)(2,1)S(1)} %shard_map.72.fb_ref, bf16[384,256]{1,0:T(8,128)(2,1)S(1)} %collective-permute-done.5.ob_ref), custom_call_target="tpu_custom_call" | custom-call | flops 1000 | bytes 1000 | tf_op jit(solution)/shard_map/pallas_call | solution.py:162
  26.2 1.1 %collective-permute-start.6 = (f16[64,512]{1,0:T(8,128)(2,1)S(1)}, f16[64,512]{1,0:T(8,128)(2,1)S(1)}, u32[]{:S(2)}, u32[]{:S(2)}) collective-permute-start(f16[64,512]{1,0:T(8,128)(2,1)S(1)} %get-tuple-element.27), channel_id=1, source_target_pairs={{0,2},{2,4},{4,6},{6,0},{1,3},{3,5},{5,7},{7,1},{8,10},{10,12},{12... | collective-permute-start | bytes 196616 | tf_op jit(solution)/shard_map/ppermute | solution.py:240
  27.3 2.9 %collective-permute-start.7 = (f16[64,512]{1,0:T(8,128)(2,1)S(1)}, f16[64,512]{1,0:T(8,128)(2,1)S(1)}, u32[]{:S(2)}, u32[]{:S(2)}) collective-permute-start(f16[64,512]{1,0:T(8,128)(2,1)S(1)} %get-tuple-element.26), channel_id=1, source_target_pairs={{0,4},{2,6},{4,0},{6,2},{1,5},{3,7},{5,1},{7,3},{8,12},{10,14},{12... | collective-permute-start | bytes 196616 | tf_op jit(solution)/shard_map/ppermute | solution.py:240
  30.2 0.0 collective-permute-start.8
  30.2 2.9 %collective-permute-done.6 = f16[64,512]{1,0:T(8,128)(2,1)S(1)} collective-permute-done((f16[64,512]{1,0:T(8,128)(2,1)S(1)}, f16[64,512]{1,0:T(8,128)(2,1)S(1)}, u32[]{:S(2)}, u32[]{:S(2)}) %collective-permute-start.6) | collective-permute-done | bytes 65568 | tf_op jit(solution)/shard_map/ppermute | solution.py:240
  33.1 0.1 shard_map.75.sum_ref
  33.2 1.8 %collective-permute-done.7 = f16[64,512]{1,0:T(8,128)(2,1)S(1)} collective-permute-done((f16[64,512]{1,0:T(8,128)(2,1)S(1)}, f16[64,512]{1,0:T(8,128)(2,1)S(1)}, u32[]{:S(2)}, u32[]{:S(2)}) %collective-permute-start.7) | collective-permute-done | bytes 65568 | tf_op jit(solution)/shard_map/ppermute | solution.py:240
  35.1 0.1 shard_map.76.sum_ref
  35.2 0.3 collective-permute-done.8
  35.4 0.9 %shard_map.77 = f32[64,512]{1,0:T(8,128)} custom-call(f32[64,512]{1,0:T(8,128)S(1)} %shard_map.76.sum_ref, f32[64,512]{1,0:T(8,128)S(1)} %convert_element_type.15.piece_ref), custom_call_target="tpu_custom_call" | custom-call | flops 1000 | bytes 1000 | tf_op jit(solution)/shard_map/pallas_call | solution.py:221
  (8 shorter events, 0.1 us)
Async XLA Ops:
  1.1 10.4 %collective-permute-start.1 = (bf16[384,256]{1,0:T(8,128)(2,1)S(1)}, bf16[384,256]{1,0:T(8,128)(2,1)S(1)}, u32[]{:S(2)}, u32[]{:S(2)}) collective-permute-start(bf16[384,256]{1,0:T(8,128)(2,1)S(1)} %get-tuple-element.24.xa_ref.x_ref), channel_id=1, source_target_pairs={{2,0},{4,2},{6,4},{0,6},{3,1},{5,3},{7,5},{1,7},{10,8},{12,10},{14... | collective-permute-start | bytes 589832 | tf_op jit(solution)/shard_map/ppermute | solution.py:259
  6.2 1.4 %copy-start = (bf16[6,6,128,128]{3,2,1,0:T(8,128)(2,1)S(1)}, bf16[6,6,128,128]{3,2,1,0:T(8,128)(2,1)}, u32[]{:S(2)}) copy-start(bf16[6,6,128,128]{3,2,1,0:T(8,128)(2,1)} %hop_ref.1) | copy-start | bytes 3538948
  6.2 1.4 %copy-start.1 = (s32[6,6]{1,0:T(8,128)S(1)}, s32[6,6]{1,0:T(8,128)}, u32[]{:S(2)}) copy-start(s32[6,6]{1,0:T(8,128)} %pattern_ref.1) | copy-start | bytes 436
  6.2 9.8 %collective-permute-start = (bf16[384,256]{1,0:T(8,128)(2,1)S(1)}, bf16[384,256]{1,0:T(8,128)(2,1)S(1)}, u32[]{:S(2)}, u32[]{:S(2)}) collective-permute-start(bf16[384,256]{1,0:T(8,128)(2,1)S(1)} %get-tuple-element.23.xb_ref.x_ref), channel_id=1, source_target_pairs={{0,2},{2,4},{4,6},{6,0},{1,3},{3,5},{5,7},{7,1},{8,10},{10,12},{12... | collective-permute-start | bytes 589832 | tf_op jit(solution)/shard_map/ppermute | solution.py:259
  11.7 10.1 %collective-permute-start.2 = (bf16[384,256]{1,0:T(8,128)(2,1)S(1)}, bf16[384,256]{1,0:T(8,128)(2,1)S(1)}, u32[]{:S(2)}, u32[]{:S(2)}) collective-permute-start(bf16[384,256]{1,0:T(8,128)(2,1)S(1)} %shard_map.67.sb_ref.s_ref), channel_id=1, source_target_pairs={{0,2},{2,4},{4,6},{6,0},{1,3},{3,5},{5,7},{7,1},{8,10},{10,12},{12... | collective-permute-start | bytes 589832 | tf_op jit(solution)/shard_map/ppermute | solution.py:259
  16.2 7.6 %collective-permute-start.3 = (bf16[384,256]{1,0:T(8,128)(2,1)S(1)}, bf16[384,256]{1,0:T(8,128)(2,1)S(1)}, u32[]{:S(2)}, u32[]{:S(2)}) collective-permute-start(bf16[384,256]{1,0:T(8,128)(2,1)S(1)} %shard_map.68.sa_ref.s_ref), channel_id=1, source_target_pairs={{2,0},{4,2},{6,4},{0,6},{3,1},{5,3},{7,5},{1,7},{10,8},{12,10},{14... | collective-permute-start | bytes 589832 | tf_op jit(solution)/shard_map/ppermute | solution.py:259
  22.2 2.1 %collective-permute-start.4 = (bf16[384,256]{1,0:T(8,128)(2,1)S(1)}, bf16[384,256]{1,0:T(8,128)(2,1)S(1)}, u32[]{:S(2)}, u32[]{:S(2)}) collective-permute-start(bf16[384,256]{1,0:T(8,128)(2,1)S(1)} %shard_map.71.fa_ref), channel_id=1, source_target_pairs={{0,1},{1,0},{2,3},{3,2},{4,5},{5,4},{6,7},{7,6},{8,9},{9,8},{10,11... | collective-permute-start | bytes 589832 | tf_op jit(solution)/shard_map/ppermute | solution.py:273
  24.1 1.5 %collective-permute-start.5 = (bf16[384,256]{1,0:T(8,128)(2,1)S(1)}, bf16[384,256]{1,0:T(8,128)(2,1)S(1)}, u32[]{:S(2)}, u32[]{:S(2)}) collective-permute-start(bf16[384,256]{1,0:T(8,128)(2,1)S(1)} %shard_map.72.fb_ref), channel_id=1, source_target_pairs={{0,1},{1,0},{2,3},{3,2},{4,5},{5,4},{6,7},{7,6},{8,9},{9,8},{10,11... | collective-permute-start | bytes 589832 | tf_op jit(solution)/shard_map/ppermute | solution.py:275
  26.2 6.9 %collective-permute-start.6 = (f16[64,512]{1,0:T(8,128)(2,1)S(1)}, f16[64,512]{1,0:T(8,128)(2,1)S(1)}, u32[]{:S(2)}, u32[]{:S(2)}) collective-permute-start(f16[64,512]{1,0:T(8,128)(2,1)S(1)} %get-tuple-element.27), channel_id=1, source_target_pairs={{0,2},{2,4},{4,6},{6,0},{1,3},{3,5},{5,7},{7,1},{8,10},{10,12},{12... | collective-permute-start | bytes 196616 | tf_op jit(solution)/shard_map/ppermute | solution.py:240
  27.3 7.8 %collective-permute-start.7 = (f16[64,512]{1,0:T(8,128)(2,1)S(1)}, f16[64,512]{1,0:T(8,128)(2,1)S(1)}, u32[]{:S(2)}, u32[]{:S(2)}) collective-permute-start(f16[64,512]{1,0:T(8,128)(2,1)S(1)} %get-tuple-element.26), channel_id=1, source_target_pairs={{0,4},{2,6},{4,0},{6,2},{1,5},{3,7},{5,1},{7,3},{8,12},{10,14},{12... | collective-permute-start | bytes 196616 | tf_op jit(solution)/shard_map/ppermute | solution.py:240
  30.2 5.2 %collective-permute-start.8 = (f16[64,512]{1,0:T(8,128)(2,1)S(1)}, f16[64,512]{1,0:T(8,128)(2,1)S(1)}, u32[]{:S(2)}, u32[]{:S(2)}) collective-permute-start(f16[64,512]{1,0:T(8,128)(2,1)S(1)} %get-tuple-element.25), channel_id=1, source_target_pairs={{0,6},{2,0},{4,2},{6,4},{1,7},{3,1},{5,3},{7,5},{8,14},{10,8},{12,... | collective-permute-start | bytes 196616 | tf_op jit(solution)/shard_map/ppermute | solution.py:240
where the time goes:
time: 36.5 us; the launch traced here: 36.4 us
  waiting for transfers between devices  16.5 us (45%)
  starting transfers between devices  11.2 us (31%)
  Pallas kernels  5.24 us (14%)
  between operations  2.26 us (6%)
  local copies, waits for them, and re-layouts  1.1 us (3%)
    ppermute x2, starting transfers between devices, halos_of(): lax.ppermute(low, 'row', backward)  6.92 us
    ppermute x2, waiting for transfers between devices, halos_of(): lax.ppermute(high, 'row', forward)  6.76 us
    ppermute x3, waiting for transfers between devices, send_shares(): arrived.append(lax.ppermute(part, 'row', ring))  4.96 us
    ppermute x3, starting transfers between devices, send_shares(): arrived.append(lax.ppermute(part, 'row', ring))  4.04 us
    ppermute x2, waiting for transfers between devices, halos_of(): lax.ppermute(low, 'row', backward)  3.96 us
    pallas_call x1, Pallas kernels, band_parts(): call(functools.partial(band_kernel, total_blocks), (jax.ShapeDtypeStruct(...  1.52 us
    slice x1, local copies, waits for them, and re-layouts, body(): xa, xb = (x[:wide], x[wide:])  1.05 us
    pallas_call x1, Pallas kernels, last_sum(): call(functools.partial(last_kernel, order_total), shape, [VMEM] * 2)  0.91 us
  transfers between devices with their start and end apart: 9, of which 8 were waited for; matrix products, arithmetic and copies ran while one was open for 0% of the time, Pallas kernels for 11%

commit v1 on v0

--- a/solution.py
+++ b/solution.py
@@ -134,32 +134,33 @@
     return jnp.where((lax.rem(row, share) == line) & (col == row - line), e, same)
 
 
-def early_kernel(share, fa_ref, fb_ref, oa_ref, out_ref):
+def early_kernel(share, fa_ref, fb_ref, oa_ref, out_ref, turned_ref):
     half = fa_ref.shape[1]
     fa, fb = fa_ref[...], fb_ref[...]
     same = tmm(fa, fa) + tmm(fb, fb)
     e = exponent(same)
     out_ref[:, :half] = with_code(share, 1, same * jnp.exp2(-e), e)
     out_ref[:, half:] = tmm(fa, oa_ref[...])
+    turned_ref[...] = fb.T
 
 
 def early_terms(fa, fb, oa, share):
     half = fa.shape[1]
-    shape = jax.ShapeDtypeStruct((half, 2 * half), jnp.float32)
-    return call(functools.partial(early_kernel, share), shape, [VMEM] * 3)(fa, fb, oa)
-
-
-def code_kernel(share, early_ref, fb_ref, ob_ref, out_ref):
-    half = fb_ref.shape[1]
-    cross = early_ref[:, half:] + tmm(fb_ref[...], ob_ref[...])
+    shapes = (jax.ShapeDtypeStruct((half, 2 * half), jnp.float32), jax.ShapeDtypeStruct(fb.shape[::-1], fb.dtype))
+    return call(functools.partial(early_kernel, share), shapes, [VMEM] * 3)(fa, fb, oa)
+
+
+def code_kernel(share, early_ref, turned_ref, ob_ref, out_ref):
+    half = turned_ref.shape[0]
+    cross = early_ref[:, half:] + mm(turned_ref[...], ob_ref[...])
     e = exponent(cross)
     out_ref[:, :half] = with_code(share, 2, early_ref[:, :half], e)
     out_ref[:, half:] = cross * jnp.exp2(-e)
 
 
-def code_terms(early, fb, ob, share):
+def code_terms(early, turned, ob, share):
     shape = jax.ShapeDtypeStruct(early.shape, jnp.float32)
-    return call(functools.partial(code_kernel, share), shape, [VMEM] * 3)(early, fb, ob)
+    return call(functools.partial(code_kernel, share), shape, [VMEM] * 3)(early, turned, ob)
 
 
 def pick(head, shift, share):
@@ -273,7 +274,8 @@
     oa = lax.ppermute(fa, "sub", swap)
     fb = finish(1, table, live, image, band, lax.optimization_barrier((halo_b, fa))[0], sb, xb)
     ob = lax.ppermute(fb, "sub", swap)
-    coded = code_terms(early_terms(fa, fb, oa, share), fb, ob, share)
+    early, turned = early_terms(fa, fb, oa, share)
+    coded = code_terms(early, turned, ob, share)
     first, *middle, last = send_shares(coded.astype(jnp.float16), row_count, share)
     total = first_sum(coded, first.astype(jnp.float32), order_total)
     for piece in middle:

time: 36.5 us -> 36.5 us (level)
  no operation moved by 1% of the time
where the time goes in v1:
time: 36.5 us; the launch traced here: 36.3 us
  waiting for transfers between devices  16.5 us (45%)
  starting transfers between devices  11.2 us (31%)
  Pallas kernels  5.21 us (14%)
  between operations  2.26 us (6%)
  local copies, waits for them, and re-layouts  1.1 us (3%)
    ppermute x2, starting transfers between devices, halos_of(): lax.ppermute(low, 'row', backward)  6.92 us
    ppermute x2, waiting for transfers between devices, halos_of(): lax.ppermute(high, 'row', forward)  6.76 us
    ppermute x3, waiting for transfers between devices, send_shares(): arrived.append(lax.ppermute(part, 'row', ring))  4.96 us
    ppermute x3, starting transfers between devices, send_shares(): arrived.append(lax.ppermute(part, 'row', ring))  4.04 us
    ppermute x2, waiting for transfers between devices, halos_of(): lax.ppermute(low, 'row', backward)  3.96 us
    pallas_call x1, Pallas kernels, band_parts(): call(functools.partial(band_kernel, total_blocks), (jax.ShapeDtypeStruct(...  1.52 us
    slice x1, local copies, waits for them, and re-layouts, body(): xa, xb = (x[:wide], x[wide:])  1.05 us
    pallas_call x1, Pallas kernels, last_sum(): call(functools.partial(last_kernel, order_total), shape, [VMEM] * 2)  0.91 us
  transfers between devices with their start and end apart: 9, of which 8 were waited for; matrix products, arithmetic and copies ran while one was open for 0% of the time, Pallas kernels for 11%

profile of v1, /device:TPU:0, one launch (start us, length us, event | category | flops | bytes accessed | tf_op | source)
XLA Modules:
  0.0 36.3 jit_solution(7897849545859742008)
XLA Ops:
  0.0 1.0 %slice_bitcast_fusion = (bf16[384,256]{1,0:T(8,128)(2,1)S(1)}, bf16[384,256]{1,0:T(8,128)(2,1)S(1)}) fusion(bf16[1,768,256]{2,1,0:T(8,128)(2,1)} %param.8), kind=kLoop, calls=%fused_computation | loop fusion | bytes 786432 | tf_op jit(solution)/shard_map/slice | solution.py:263
  1.1 5.1 %collective-permute-start.1 = (bf16[384,256]{1,0:T(8,128)(2,1)S(1)}, bf16[384,256]{1,0:T(8,128)(2,1)S(1)}, u32[]{:S(2)}, u32[]{:S(2)}) collective-permute-start(bf16[384,256]{1,0:T(8,128)(2,1)S(1)} %get-tuple-element.28.xa_ref.x_ref), channel_id=1, source_target_pairs={{2,0},{4,2},{6,4},{0,6},{3,1},{5,3},{7,5},{1,7},{10,8},{12,10},{14... | collective-permute-start | bytes 589832 | tf_op jit(solution)/shard_map/ppermute | solution.py:260
  6.2 0.0 copy-start
  6.2 0.0 copy-start.1
  6.2 0.0 collective-permute-start
  7.6 0.0 copy-done
  7.6 0.0 copy-done.1
  7.6 1.5 %shard_map.66 = (bf16[768,1152]{1,0:T(8,128)(2,1)S(1)}, f32[768,256]{1,0:T(8,128)S(1)}) custom-call(f32[8,256]{1,0:T(8,128)S(1)} %shard_map.65.table_ref, s32[6,6]{1,0:T(8,128)S(1)} %copy-done.1, bf16[6,6,128,128]{3,2,1,0:T(8,128)(2,1)S(1)} %copy-done, bf16[384,256]{1,0:T(8,128)(2,1)S(1)} %get-tuple-element.28.xa_ref.x_ref, ...), custom_call_target="tpu_custom_call" | custom-call | flops 1000 | bytes 1000 | tf_op jit(solution)/shard_map/pallas_call | solution.py:86
  9.1 2.3 %collective-permute-done.1.halo_ref = bf16[384,256]{1,0:T(8,128)(2,1)S(1)} collective-permute-done((bf16[384,256]{1,0:T(8,128)(2,1)S(1)}, bf16[384,256]{1,0:T(8,128)(2,1)S(1)}, u32[]{:S(2)}, u32[]{:S(2)}) %collective-permute-start.1) | collective-permute-done | bytes 196640 | tf_op jit(solution)/shard_map/ppermute | solution.py:260
  11.5 0.3 shard_map.67.sb_ref.s_ref
  11.7 0.1 collective-permute-start.2
  11.8 4.2 %collective-permute-done.halo_ref = bf16[384,256]{1,0:T(8,128)(2,1)S(1)} collective-permute-done((bf16[384,256]{1,0:T(8,128)(2,1)S(1)}, bf16[384,256]{1,0:T(8,128)(2,1)S(1)}, u32[]{:S(2)}, u32[]{:S(2)}) %collective-permute-start) | collective-permute-done | bytes 196640 | tf_op jit(solution)/shard_map/ppermute | solution.py:260
  16.0 0.3 shard_map.68.sa_ref.s_ref
  16.2 1.8 %collective-permute-start.3 = (bf16[384,256]{1,0:T(8,128)(2,1)S(1)}, bf16[384,256]{1,0:T(8,128)(2,1)S(1)}, u32[]{:S(2)}, u32[]{:S(2)}) collective-permute-start(bf16[384,256]{1,0:T(8,128)(2,1)S(1)} %shard_map.68.sa_ref.s_ref), channel_id=1, source_target_pairs={{2,0},{4,2},{6,4},{0,6},{3,1},{5,3},{7,5},{1,7},{10,8},{12,10},{14... | collective-permute-start | bytes 589832 | tf_op jit(solution)/shard_map/ppermute | solution.py:260
  18.7 0.6 %shard_map.70.image_ref = f32[768,256]{1,0:T(8,128)S(1)} custom-call(bf16[768,1152]{1,0:T(8,128)(2,1)S(1)} %get-tuple-element.19.band_ref, bf16[384,256]{1,0:T(8,128)(2,1)S(1)} %shard_map.68.sa_ref.s_ref, bf16[384,256]{1,0:T(8,128)(2,1)S(1)} %shard_map.67.sb_ref.s_ref), custom_call_target="tpu_custom_call" | custom-call | flops 1000 | bytes 1000 | tf_op jit(solution)/shard_map/pallas_call | solution.py:232
  19.3 2.6 %collective-permute-done.2.halo_ref = bf16[384,256]{1,0:T(8,128)(2,1)S(1)} collective-permute-done((bf16[384,256]{1,0:T(8,128)(2,1)S(1)}, bf16[384,256]{1,0:T(8,128)(2,1)S(1)}, u32[]{:S(2)}, u32[]{:S(2)}) %collective-permute-start.2) | collective-permute-done | bytes 196640 | tf_op jit(solution)/shard_map/ppermute | solution.py:260
  21.9 0.3 shard_map.71.fa_ref
  22.2 0.1 collective-permute-start.4
  22.2 1.6 %collective-permute-done.3.halo_ref = bf16[384,256]{1,0:T(8,128)(2,1)S(1)} collective-permute-done((bf16[384,256]{1,0:T(8,128)(2,1)S(1)}, bf16[384,256]{1,0:T(8,128)(2,1)S(1)}, u32[]{:S(2)}, u32[]{:S(2)}) %collective-permute-start.3) | collective-permute-done | bytes 196640 | tf_op jit(solution)/shard_map/ppermute | solution.py:260
  23.9 0.3 shard_map.72.fb_ref
  24.1 0.1 collective-permute-start.5
  24.3 0.0 collective-permute-done.4.oa_ref
  24.3 0.5 %shard_map.73 = (f32[256,512]{1,0:T(8,128)S(1)}, bf16[256,384]{1,0:T(8,128)(2,1)S(1)}) custom-call(bf16[384,256]{1,0:T(8,128)(2,1)S(1)} %shard_map.71.fa_ref, bf16[384,256]{1,0:T(8,128)(2,1)S(1)} %shard_map.72.fb_ref, bf16[384,256]{1,0:T(8,128)(2,1)S(1)} %collective-permute-done.4.oa_ref), custom_call_target="tpu_custom_call" | custom-call | flops 1000 | bytes 1000 | tf_op jit(solution)/shard_map/pallas_call | solution.py:150
  24.8 0.8 %collective-permute-done.5.ob_ref = bf16[384,256]{1,0:T(8,128)(2,1)S(1)} collective-permute-done((bf16[384,256]{1,0:T(8,128)(2,1)S(1)}, bf16[384,256]{1,0:T(8,128)(2,1)S(1)}, u32[]{:S(2)}, u32[]{:S(2)}) %collective-permute-start.5) | collective-permute-done | bytes 196640 | tf_op jit(solution)/shard_map/ppermute | solution.py:276
  25.6 0.4 %shard_map.74.coded_ref = f32[256,512]{1,0:T(8,128)S(1)} custom-call(f32[256,512]{1,0:T(8,128)S(1)} %get-tuple-element.23.early_ref, bf16[256,384]{1,0:T(8,128)(2,1)S(1)} %get-tuple-element.24.turned_ref, bf16[384,256]{1,0:T(8,128)(2,1)S(1)} %collective-permute-done.5.ob_ref), custom_call_target="tpu_custom_call" | custom-call | flops 1000 | bytes 1000 | tf_op jit(solution)/shard_map/pallas_call | solution.py:163
  26.1 1.1 %collective-permute-start.6 = (f16[64,512]{1,0:T(8,128)(2,1)S(1)}, f16[64,512]{1,0:T(8,128)(2,1)S(1)}, u32[]{:S(2)}, u32[]{:S(2)}) collective-permute-start(f16[64,512]{1,0:T(8,128)(2,1)S(1)} %get-tuple-element.31), channel_id=1, source_target_pairs={{0,2},{2,4},{4,6},{6,0},{1,3},{3,5},{5,7},{7,1},{8,10},{10,12},{12... | collective-permute-start | bytes 196616 | tf_op jit(solution)/shard_map/ppermute | solution.py:241
  27.2 2.9 %collective-permute-start.7 = (f16[64,512]{1,0:T(8,128)(2,1)S(1)}, f16[64,512]{1,0:T(8,128)(2,1)S(1)}, u32[]{:S(2)}, u32[]{:S(2)}) collective-permute-start(f16[64,512]{1,0:T(8,128)(2,1)S(1)} %get-tuple-element.30), channel_id=1, source_target_pairs={{0,4},{2,6},{4,0},{6,2},{1,5},{3,7},{5,1},{7,3},{8,12},{10,14},{12... | collective-permute-start | bytes 196616 | tf_op jit(solution)/shard_map/ppermute | solution.py:241
  30.2 0.0 collective-permute-start.8
  30.2 2.9 %collective-permute-done.6 = f16[64,512]{1,0:T(8,128)(2,1)S(1)} collective-permute-done((f16[64,512]{1,0:T(8,128)(2,1)S(1)}, f16[64,512]{1,0:T(8,128)(2,1)S(1)}, u32[]{:S(2)}, u32[]{:S(2)}) %collective-permute-start.6) | collective-permute-done | bytes 65568 | tf_op jit(solution)/shard_map/ppermute | solution.py:241
  33.1 0.1 shard_map.75.sum_ref
  33.2 1.8 %collective-permute-done.7 = f16[64,512]{1,0:T(8,128)(2,1)S(1)} collective-permute-done((f16[64,512]{1,0:T(8,128)(2,1)S(1)}, f16[64,512]{1,0:T(8,128)(2,1)S(1)}, u32[]{:S(2)}, u32[]{:S(2)}) %collective-permute-start.7) | collective-permute-done | bytes 65568 | tf_op jit(solution)/shard_map/ppermute | solution.py:241
  35.0 0.1 shard_map.76.sum_ref
  35.1 0.3 collective-permute-done.8
  35.4 0.9 %shard_map.77 = f32[64,512]{1,0:T(8,128)} custom-call(f32[64,512]{1,0:T(8,128)S(1)} %shard_map.76.sum_ref, f32[64,512]{1,0:T(8,128)S(1)} %convert_element_type.15.piece_ref), custom_call_target="tpu_custom_call" | custom-call | flops 1000 | bytes 1000 | tf_op jit(solution)/shard_map/pallas_call | solution.py:222
  (8 shorter events, 0.1 us)
Async XLA Ops:
  1.1 10.4 %collective-permute-start.1 = (bf16[384,256]{1,0:T(8,128)(2,1)S(1)}, bf16[384,256]{1,0:T(8,128)(2,1)S(1)}, u32[]{:S(2)}, u32[]{:S(2)}) collective-permute-start(bf16[384,256]{1,0:T(8,128)(2,1)S(1)} %get-tuple-element.28.xa_ref.x_ref), channel_id=1, source_target_pairs={{2,0},{4,2},{6,4},{0,6},{3,1},{5,3},{7,5},{1,7},{10,8},{12,10},{14... | collective-permute-start | bytes 589832 | tf_op jit(solution)/shard_map/ppermute | solution.py:260
  6.2 1.4 %copy-start = (bf16[6,6,128,128]{3,2,1,0:T(8,128)(2,1)S(1)}, bf16[6,6,128,128]{3,2,1,0:T(8,128)(2,1)}, u32[]{:S(2)}) copy-start(bf16[6,6,128,128]{3,2,1,0:T(8,128)(2,1)} %hop_ref.1) | copy-start | bytes 3538948
  6.2 1.4 %copy-start.1 = (s32[6,6]{1,0:T(8,128)S(1)}, s32[6,6]{1,0:T(8,128)}, u32[]{:S(2)}) copy-start(s32[6,6]{1,0:T(8,128)} %pattern_ref.1) | copy-start | bytes 436
  6.2 9.8 %collective-permute-start = (bf16[384,256]{1,0:T(8,128)(2,1)S(1)}, bf16[384,256]{1,0:T(8,128)(2,1)S(1)}, u32[]{:S(2)}, u32[]{:S(2)}) collective-permute-start(bf16[384,256]{1,0:T(8,128)(2,1)S(1)} %get-tuple-element.27.xb_ref.x_ref), channel_id=1, source_target_pairs={{0,2},{2,4},{4,6},{6,0},{1,3},{3,5},{5,7},{7,1},{8,10},{10,12},{12... | collective-permute-start | bytes 589832 | tf_op jit(solution)/shard_map/ppermute | solution.py:260
  11.7 10.1 %collective-permute-start.2 = (bf16[384,256]{1,0:T(8,128)(2,1)S(1)}, bf16[384,256]{1,0:T(8,128)(2,1)S(1)}, u32[]{:S(2)}, u32[]{:S(2)}) collective-permute-start(bf16[384,256]{1,0:T(8,128)(2,1)S(1)} %shard_map.67.sb_ref.s_ref), channel_id=1, source_target_pairs={{0,2},{2,4},{4,6},{6,0},{1,3},{3,5},{5,7},{7,1},{8,10},{10,12},{12... | collective-permute-start | bytes 589832 | tf_op jit(solution)/shard_map/ppermute | solution.py:260
  16.2 7.6 %collective-permute-start.3 = (bf16[384,256]{1,0:T(8,128)(2,1)S(1)}, bf16[384,256]{1,0:T(8,128)(2,1)S(1)}, u32[]{:S(2)}, u32[]{:S(2)}) collective-permute-start(bf16[384,256]{1,0:T(8,128)(2,1)S(1)} %shard_map.68.sa_ref.s_ref), channel_id=1, source_target_pairs={{2,0},{4,2},{6,4},{0,6},{3,1},{5,3},{7,5},{1,7},{10,8},{12,10},{14... | collective-permute-start | bytes 589832 | tf_op jit(solution)/shard_map/ppermute | solution.py:260
  22.2 2.1 %collective-permute-start.4 = (bf16[384,256]{1,0:T(8,128)(2,1)S(1)}, bf16[384,256]{1,0:T(8,128)(2,1)S(1)}, u32[]{:S(2)}, u32[]{:S(2)}) collective-permute-start(bf16[384,256]{1,0:T(8,128)(2,1)S(1)} %shard_map.71.fa_ref), channel_id=1, source_target_pairs={{0,1},{1,0},{2,3},{3,2},{4,5},{5,4},{6,7},{7,6},{8,9},{9,8},{10,11... | collective-permute-start | bytes 589832 | tf_op jit(solution)/shard_map/ppermute | solution.py:274
  24.1 1.5 %collective-permute-start.5 = (bf16[384,256]{1,0:T(8,128)(2,1)S(1)}, bf16[384,256]{1,0:T(8,128)(2,1)S(1)}, u32[]{:S(2)}, u32[]{:S(2)}) collective-permute-start(bf16[384,256]{1,0:T(8,128)(2,1)S(1)} %shard_map.72.fb_ref), channel_id=1, source_target_pairs={{0,1},{1,0},{2,3},{3,2},{4,5},{5,4},{6,7},{7,6},{8,9},{9,8},{10,11... | collective-permute-start | bytes 589832 | tf_op jit(solution)/shard_map/ppermute | solution.py:276
  26.1 6.9 %collective-permute-start.6 = (f16[64,512]{1,0:T(8,128)(2,1)S(1)}, f16[64,512]{1,0:T(8,128)(2,1)S(1)}, u32[]{:S(2)}, u32[]{:S(2)}) collective-permute-start(f16[64,512]{1,0:T(8,128)(2,1)S(1)} %get-tuple-element.31), channel_id=1, source_target_pairs={{0,2},{2,4},{4,6},{6,0},{1,3},{3,5},{5,7},{7,1},{8,10},{10,12},{12... | collective-permute-start | bytes 196616 | tf_op jit(solution)/shard_map/ppermute | solution.py:241
  27.2 7.8 %collective-permute-start.7 = (f16[64,512]{1,0:T(8,128)(2,1)S(1)}, f16[64,512]{1,0:T(8,128)(2,1)S(1)}, u32[]{:S(2)}, u32[]{:S(2)}) collective-permute-start(f16[64,512]{1,0:T(8,128)(2,1)S(1)} %get-tuple-element.30), channel_id=1, source_target_pairs={{0,4},{2,6},{4,0},{6,2},{1,5},{3,7},{5,1},{7,3},{8,12},{10,14},{12... | collective-permute-start | bytes 196616 | tf_op jit(solution)/shard_map/ppermute | solution.py:241
  30.2 5.2 %collective-permute-start.8 = (f16[64,512]{1,0:T(8,128)(2,1)S(1)}, f16[64,512]{1,0:T(8,128)(2,1)S(1)}, u32[]{:S(2)}, u32[]{:S(2)}) collective-permute-start(f16[64,512]{1,0:T(8,128)(2,1)S(1)} %get-tuple-element.29), channel_id=1, source_target_pairs={{0,6},{2,0},{4,2},{6,4},{1,7},{3,1},{5,3},{7,5},{8,14},{10,8},{12,... | collective-permute-start | bytes 196616 | tf_op jit(solution)/shard_map/ppermute | solution.py:241

commit v2 on v1

--- a/solution.py
+++ b/solution.py
@@ -200,26 +200,46 @@
     return call(functools.partial(add_kernel, order_total), shape, [VMEM] * 2, LONG)(total, piece)
 
 
-def last_kernel(order_total, sum_ref, piece_ref, out_ref):
-    share, half = out_ref.shape[0], out_ref.shape[1] // 2
+def last_kernel(order_total, sum_ref, piece_ref, out_any, held_ref, sems):
+    _, share, half = held_ref.shape
     same, cross = factors(piece_ref[:8, :half], share, order_total)
     sub = lax.axis_index("sub")
-    at = pl.ds(pl.multiple_of(sub * half, half), half)
-    other = pl.ds(pl.multiple_of((1 - sub) * half, half), half)
-    out_ref[:, other] = sum_ref[:, half:] + piece_ref[:, half:] * cross
-    out_ref[:, at] = sum_ref[:, :half] + piece_ref[:, :half] * same
+
+    def leave(slot, place):
+        columns = pl.ds(pl.multiple_of(place * half, half), half)
+        return pltpu.make_async_copy(held_ref.at[slot], out_any.at[:, columns], sems.at[slot])
+
+    held_ref[0] = sum_ref[:, half:] + piece_ref[:, half:] * cross
+    cross_copy = leave(0, 1 - sub)
+    cross_copy.start()
+    held_ref[1] = sum_ref[:, :half] + piece_ref[:, :half] * same
     head = sum_ref[:8, :half] + piece_ref[:8, :half] * same
     row = lax.broadcasted_iota(jnp.int32, head.shape, 0)
     col = lax.broadcasted_iota(jnp.int32, head.shape, 1)
     start = col == lax.axis_index("row") * share
     for line in (1, 2):
         head = jnp.where((row == line) & start, pick(head[:1], line, share), head)
-    out_ref[:8, at] = head
+    held_ref[1, :8, :] = head
+    same_copy = leave(1, sub)
+    same_copy.start()
+    cross_copy.wait()
+    same_copy.wait()
 
 
 def last_sum(total, piece, order_total):
-    shape = jax.ShapeDtypeStruct(total.shape, jnp.float32)
-    return call(functools.partial(last_kernel, order_total), shape, [VMEM] * 2)(total, piece)
+    share, columns = total.shape
+    return pl.pallas_call(
+        functools.partial(last_kernel, order_total),
+        out_shape=jax.ShapeDtypeStruct(total.shape, jnp.float32),
+        in_specs=[VMEM] * 2,
+        out_specs=pl.BlockSpec(memory_space=pl.ANY),
+        scratch_shapes=[
+            pltpu.VMEM((2, share, columns // 2), jnp.float32),
+            pltpu.SemaphoreType.DMA((2,)),
+        ],
+        compiler_params=pltpu.CompilerParams(vmem_limit_bytes=LIMIT),
+        cost_estimate=COST,
+    )(total, piece)
 
 
 def image_kernel(band_ref, sa_ref, sb_ref, out_ref):

time: 36.5 us -> 36.5 us (level)
  no operation moved by 1% of the time
where the time goes in v2:
time: 36.5 us; the launch traced here: 36.3 us
  waiting for transfers between devices  16.5 us (45%)
  starting transfers between devices  11.2 us (31%)
  Pallas kernels  5.21 us (14%)
  between operations  2.26 us (6%)
  local copies, waits for them, and re-layouts  1.1 us (3%)
    ppermute x2, starting transfers between devices, halos_of(): lax.ppermute(low, 'row', backward)  6.92 us
    ppermute x2, waiting for transfers between devices, halos_of(): lax.ppermute(high, 'row', forward)  6.76 us
    ppermute x3, waiting for transfers between devices, send_shares(): arrived.append(lax.ppermute(part, 'row', ring))  4.96 us
    ppermute x3, starting transfers between devices, send_shares(): arrived.append(lax.ppermute(part, 'row', ring))  4.04 us
    ppermute x2, waiting for transfers between devices, halos_of(): lax.ppermute(low, 'row', backward)  3.96 us
    pallas_call x1, Pallas kernels, band_parts(): call(functools.partial(band_kernel, total_blocks), (jax.ShapeDtypeStruct(...  1.52 us
    slice x1, local copies, waits for them, and re-layouts, body(): xa, xb = (x[:wide], x[wide:])  1.05 us
    pallas_call x1, Pallas kernels, last_sum(): pl.pallas_call(functools.partial(last_kernel, order_total), out_shape=jax...  0.91 us
  transfers between devices with their start and end apart: 9, of which 8 were waited for; matrix products, arithmetic and copies ran while one was open for 0% of the time, Pallas kernels for 11%

profile of v2, /device:TPU:0, one launch (start us, length us, event | category | flops | bytes accessed | tf_op | source)
XLA Modules:
  0.0 36.3 jit_solution(11538129190139520086)
XLA Ops:
  0.0 1.0 %slice_bitcast_fusion = (bf16[384,256]{1,0:T(8,128)(2,1)S(1)}, bf16[384,256]{1,0:T(8,128)(2,1)S(1)}) fusion(bf16[1,768,256]{2,1,0:T(8,128)(2,1)} %param.8), kind=kLoop, calls=%fused_computation | loop fusion | bytes 786432 | tf_op jit(solution)/shard_map/slice | solution.py:283
  1.1 5.1 %collective-permute-start.1 = (bf16[384,256]{1,0:T(8,128)(2,1)S(1)}, bf16[384,256]{1,0:T(8,128)(2,1)S(1)}, u32[]{:S(2)}, u32[]{:S(2)}) collective-permute-start(bf16[384,256]{1,0:T(8,128)(2,1)S(1)} %get-tuple-element.28.xa_ref.x_ref), channel_id=1, source_target_pairs={{2,0},{4,2},{6,4},{0,6},{3,1},{5,3},{7,5},{1,7},{10,8},{12,10},{14... | collective-permute-start | bytes 589832 | tf_op jit(solution)/shard_map/ppermute | solution.py:280
  6.2 0.0 copy-start
  6.2 0.0 copy-start.1
  6.2 0.0 collective-permute-start
  7.6 0.0 copy-done
  7.6 0.0 copy-done.1
  7.6 1.5 %shard_map.66 = (bf16[768,1152]{1,0:T(8,128)(2,1)S(1)}, f32[768,256]{1,0:T(8,128)S(1)}) custom-call(f32[8,256]{1,0:T(8,128)S(1)} %shard_map.65.table_ref, s32[6,6]{1,0:T(8,128)S(1)} %copy-done.1, bf16[6,6,128,128]{3,2,1,0:T(8,128)(2,1)S(1)} %copy-done, bf16[384,256]{1,0:T(8,128)(2,1)S(1)} %get-tuple-element.28.xa_ref.x_ref, ...), custom_call_target="tpu_custom_call" | custom-call | flops 1000 | bytes 1000 | tf_op jit(solution)/shard_map/pallas_call | solution.py:86
  9.1 2.3 %collective-permute-done.1.halo_ref = bf16[384,256]{1,0:T(8,128)(2,1)S(1)} collective-permute-done((bf16[384,256]{1,0:T(8,128)(2,1)S(1)}, bf16[384,256]{1,0:T(8,128)(2,1)S(1)}, u32[]{:S(2)}, u32[]{:S(2)}) %collective-permute-start.1) | collective-permute-done | bytes 196640 | tf_op jit(solution)/shard_map/ppermute | solution.py:280
  11.5 0.3 shard_map.67.sb_ref.s_ref
  11.7 0.1 collective-permute-start.2
  11.8 4.2 %collective-permute-done.halo_ref = bf16[384,256]{1,0:T(8,128)(2,1)S(1)} collective-permute-done((bf16[384,256]{1,0:T(8,128)(2,1)S(1)}, bf16[384,256]{1,0:T(8,128)(2,1)S(1)}, u32[]{:S(2)}, u32[]{:S(2)}) %collective-permute-start) | collective-permute-done | bytes 196640 | tf_op jit(solution)/shard_map/ppermute | solution.py:280
  16.0 0.3 shard_map.68.sa_ref.s_ref
  16.2 1.8 %collective-permute-start.3 = (bf16[384,256]{1,0:T(8,128)(2,1)S(1)}, bf16[384,256]{1,0:T(8,128)(2,1)S(1)}, u32[]{:S(2)}, u32[]{:S(2)}) collective-permute-start(bf16[384,256]{1,0:T(8,128)(2,1)S(1)} %shard_map.68.sa_ref.s_ref), channel_id=1, source_target_pairs={{2,0},{4,2},{6,4},{0,6},{3,1},{5,3},{7,5},{1,7},{10,8},{12,10},{14... | collective-permute-start | bytes 589832 | tf_op jit(solution)/shard_map/ppermute | solution.py:280
  18.7 0.6 %shard_map.70.image_ref = f32[768,256]{1,0:T(8,128)S(1)} custom-call(bf16[768,1152]{1,0:T(8,128)(2,1)S(1)} %get-tuple-element.19.band_ref, bf16[384,256]{1,0:T(8,128)(2,1)S(1)} %shard_map.68.sa_ref.s_ref, bf16[384,256]{1,0:T(8,128)(2,1)S(1)} %shard_map.67.sb_ref.s_ref), custom_call_target="tpu_custom_call" | custom-call | flops 1000 | bytes 1000 | tf_op jit(solution)/shard_map/pallas_call | solution.py:252
  19.3 2.6 %collective-permute-done.2.halo_ref = bf16[384,256]{1,0:T(8,128)(2,1)S(1)} collective-permute-done((bf16[384,256]{1,0:T(8,128)(2,1)S(1)}, bf16[384,256]{1,0:T(8,128)(2,1)S(1)}, u32[]{:S(2)}, u32[]{:S(2)}) %collective-permute-start.2) | collective-permute-done | bytes 196640 | tf_op jit(solution)/shard_map/ppermute | solution.py:280
  21.9 0.3 shard_map.71.fa_ref
  22.2 0.1 collective-permute-start.4
  22.2 1.6 %collective-permute-done.3.halo_ref = bf16[384,256]{1,0:T(8,128)(2,1)S(1)} collective-permute-done((bf16[384,256]{1,0:T(8,128)(2,1)S(1)}, bf16[384,256]{1,0:T(8,128)(2,1)S(1)}, u32[]{:S(2)}, u32[]{:S(2)}) %collective-permute-start.3) | collective-permute-done | bytes 196640 | tf_op jit(solution)/shard_map/ppermute | solution.py:280
  23.9 0.3 shard_map.72.fb_ref
  24.1 0.1 collective-permute-start.5
  24.3 0.0 collective-permute-done.4.oa_ref
  24.3 0.5 %shard_map.73 = (f32[256,512]{1,0:T(8,128)S(1)}, bf16[256,384]{1,0:T(8,128)(2,1)S(1)}) custom-call(bf16[384,256]{1,0:T(8,128)(2,1)S(1)} %shard_map.71.fa_ref, bf16[384,256]{1,0:T(8,128)(2,1)S(1)} %shard_map.72.fb_ref, bf16[384,256]{1,0:T(8,128)(2,1)S(1)} %collective-permute-done.4.oa_ref), custom_call_target="tpu_custom_call" | custom-call | flops 1000 | bytes 1000 | tf_op jit(solution)/shard_map/pallas_call | solution.py:150
  24.8 0.8 %collective-permute-done.5.ob_ref = bf16[384,256]{1,0:T(8,128)(2,1)S(1)} collective-permute-done((bf16[384,256]{1,0:T(8,128)(2,1)S(1)}, bf16[384,256]{1,0:T(8,128)(2,1)S(1)}, u32[]{:S(2)}, u32[]{:S(2)}) %collective-permute-start.5) | collective-permute-done | bytes 196640 | tf_op jit(solution)/shard_map/ppermute | solution.py:296
  25.6 0.4 %shard_map.74.coded_ref = f32[256,512]{1,0:T(8,128)S(1)} custom-call(f32[256,512]{1,0:T(8,128)S(1)} %get-tuple-element.23.early_ref, bf16[256,384]{1,0:T(8,128)(2,1)S(1)} %get-tuple-element.24.turned_ref, bf16[384,256]{1,0:T(8,128)(2,1)S(1)} %collective-permute-done.5.ob_ref), custom_call_target="tpu_custom_call" | custom-call | flops 1000 | bytes 1000 | tf_op jit(solution)/shard_map/pallas_call | solution.py:163
  26.1 1.1 %collective-permute-start.6 = (f16[64,512]{1,0:T(8,128)(2,1)S(1)}, f16[64,512]{1,0:T(8,128)(2,1)S(1)}, u32[]{:S(2)}, u32[]{:S(2)}) collective-permute-start(f16[64,512]{1,0:T(8,128)(2,1)S(1)} %get-tuple-element.31), channel_id=1, source_target_pairs={{0,2},{2,4},{4,6},{6,0},{1,3},{3,5},{5,7},{7,1},{8,10},{10,12},{12... | collective-permute-start | bytes 196616 | tf_op jit(solution)/shard_map/ppermute | solution.py:261
  27.2 2.9 %collective-permute-start.7 = (f16[64,512]{1,0:T(8,128)(2,1)S(1)}, f16[64,512]{1,0:T(8,128)(2,1)S(1)}, u32[]{:S(2)}, u32[]{:S(2)}) collective-permute-start(f16[64,512]{1,0:T(8,128)(2,1)S(1)} %get-tuple-element.30), channel_id=1, source_target_pairs={{0,4},{2,6},{4,0},{6,2},{1,5},{3,7},{5,1},{7,3},{8,12},{10,14},{12... | collective-permute-start | bytes 196616 | tf_op jit(solution)/shard_map/ppermute | solution.py:261
  30.2 0.0 collective-permute-start.8
  30.2 2.9 %collective-permute-done.6 = f16[64,512]{1,0:T(8,128)(2,1)S(1)} collective-permute-done((f16[64,512]{1,0:T(8,128)(2,1)S(1)}, f16[64,512]{1,0:T(8,128)(2,1)S(1)}, u32[]{:S(2)}, u32[]{:S(2)}) %collective-permute-start.6) | collective-permute-done | bytes 65568 | tf_op jit(solution)/shard_map/ppermute | solution.py:261
  33.1 0.1 shard_map.75.sum_ref
  33.2 1.8 %collective-permute-done.7 = f16[64,512]{1,0:T(8,128)(2,1)S(1)} collective-permute-done((f16[64,512]{1,0:T(8,128)(2,1)S(1)}, f16[64,512]{1,0:T(8,128)(2,1)S(1)}, u32[]{:S(2)}, u32[]{:S(2)}) %collective-permute-start.7) | collective-permute-done | bytes 65568 | tf_op jit(solution)/shard_map/ppermute | solution.py:261
  35.0 0.1 shard_map.76.sum_ref
  35.1 0.3 collective-permute-done.8
  35.4 0.9 %shard_map.77 = f32[64,512]{1,0:T(8,128)} custom-call(f32[64,512]{1,0:T(8,128)S(1)} %shard_map.76.sum_ref, f32[64,512]{1,0:T(8,128)S(1)} %convert_element_type.15.piece_ref), custom_call_target="tpu_custom_call" | custom-call | flops 1000 | bytes 1000 | tf_op jit(solution)/shard_map/pallas_call | solution.py:231
  (8 shorter events, 0.1 us)
Async XLA Ops:
  1.1 10.4 %collective-permute-start.1 = (bf16[384,256]{1,0:T(8,128)(2,1)S(1)}, bf16[384,256]{1,0:T(8,128)(2,1)S(1)}, u32[]{:S(2)}, u32[]{:S(2)}) collective-permute-start(bf16[384,256]{1,0:T(8,128)(2,1)S(1)} %get-tuple-element.28.xa_ref.x_ref), channel_id=1, source_target_pairs={{2,0},{4,2},{6,4},{0,6},{3,1},{5,3},{7,5},{1,7},{10,8},{12,10},{14... | collective-permute-start | bytes 589832 | tf_op jit(solution)/shard_map/ppermute | solution.py:280
  6.2 1.4 %copy-start = (bf16[6,6,128,128]{3,2,1,0:T(8,128)(2,1)S(1)}, bf16[6,6,128,128]{3,2,1,0:T(8,128)(2,1)}, u32[]{:S(2)}) copy-start(bf16[6,6,128,128]{3,2,1,0:T(8,128)(2,1)} %hop_ref.1) | copy-start | bytes 3538948
  6.2 1.4 %copy-start.1 = (s32[6,6]{1,0:T(8,128)S(1)}, s32[6,6]{1,0:T(8,128)}, u32[]{:S(2)}) copy-start(s32[6,6]{1,0:T(8,128)} %pattern_ref.1) | copy-start | bytes 436
  6.2 9.8 %collective-permute-start = (bf16[384,256]{1,0:T(8,128)(2,1)S(1)}, bf16[384,256]{1,0:T(8,128)(2,1)S(1)}, u32[]{:S(2)}, u32[]{:S(2)}) collective-permute-start(bf16[384,256]{1,0:T(8,128)(2,1)S(1)} %get-tuple-element.27.xb_ref.x_ref), channel_id=1, source_target_pairs={{0,2},{2,4},{4,6},{6,0},{1,3},{3,5},{5,7},{7,1},{8,10},{10,12},{12... | collective-permute-start | bytes 589832 | tf_op jit(solution)/shard_map/ppermute | solution.py:280
  11.7 10.1 %collective-permute-start.2 = (bf16[384,256]{1,0:T(8,128)(2,1)S(1)}, bf16[384,256]{1,0:T(8,128)(2,1)S(1)}, u32[]{:S(2)}, u32[]{:S(2)}) collective-permute-start(bf16[384,256]{1,0:T(8,128)(2,1)S(1)} %shard_map.67.sb_ref.s_ref), channel_id=1, source_target_pairs={{0,2},{2,4},{4,6},{6,0},{1,3},{3,5},{5,7},{7,1},{8,10},{10,12},{12... | collective-permute-start | bytes 589832 | tf_op jit(solution)/shard_map/ppermute | solution.py:280
  16.2 7.6 %collective-permute-start.3 = (bf16[384,256]{1,0:T(8,128)(2,1)S(1)}, bf16[384,256]{1,0:T(8,128)(2,1)S(1)}, u32[]{:S(2)}, u32[]{:S(2)}) collective-permute-start(bf16[384,256]{1,0:T(8,128)(2,1)S(1)} %shard_map.68.sa_ref.s_ref), channel_id=1, source_target_pairs={{2,0},{4,2},{6,4},{0,6},{3,1},{5,3},{7,5},{1,7},{10,8},{12,10},{14... | collective-permute-start | bytes 589832 | tf_op jit(solution)/shard_map/ppermute | solution.py:280
  22.2 2.1 %collective-permute-start.4 = (bf16[384,256]{1,0:T(8,128)(2,1)S(1)}, bf16[384,256]{1,0:T(8,128)(2,1)S(1)}, u32[]{:S(2)}, u32[]{:S(2)}) collective-permute-start(bf16[384,256]{1,0:T(8,128)(2,1)S(1)} %shard_map.71.fa_ref), channel_id=1, source_target_pairs={{0,1},{1,0},{2,3},{3,2},{4,5},{5,4},{6,7},{7,6},{8,9},{9,8},{10,11... | collective-permute-start | bytes 589832 | tf_op jit(solution)/shard_map/ppermute | solution.py:294
  24.1 1.5 %collective-permute-start.5 = (bf16[384,256]{1,0:T(8,128)(2,1)S(1)}, bf16[384,256]{1,0:T(8,128)(2,1)S(1)}, u32[]{:S(2)}, u32[]{:S(2)}) collective-permute-start(bf16[384,256]{1,0:T(8,128)(2,1)S(1)} %shard_map.72.fb_ref), channel_id=1, source_target_pairs={{0,1},{1,0},{2,3},{3,2},{4,5},{5,4},{6,7},{7,6},{8,9},{9,8},{10,11... | collective-permute-start | bytes 589832 | tf_op jit(solution)/shard_map/ppermute | solution.py:296
  26.1 6.9 %collective-permute-start.6 = (f16[64,512]{1,0:T(8,128)(2,1)S(1)}, f16[64,512]{1,0:T(8,128)(2,1)S(1)}, u32[]{:S(2)}, u32[]{:S(2)}) collective-permute-start(f16[64,512]{1,0:T(8,128)(2,1)S(1)} %get-tuple-element.31), channel_id=1, source_target_pairs={{0,2},{2,4},{4,6},{6,0},{1,3},{3,5},{5,7},{7,1},{8,10},{10,12},{12... | collective-permute-start | bytes 196616 | tf_op jit(solution)/shard_map/ppermute | solution.py:261
  27.2 7.8 %collective-permute-start.7 = (f16[64,512]{1,0:T(8,128)(2,1)S(1)}, f16[64,512]{1,0:T(8,128)(2,1)S(1)}, u32[]{:S(2)}, u32[]{:S(2)}) collective-permute-start(f16[64,512]{1,0:T(8,128)(2,1)S(1)} %get-tuple-element.30), channel_id=1, source_target_pairs={{0,4},{2,6},{4,0},{6,2},{1,5},{3,7},{5,1},{7,3},{8,12},{10,14},{12... | collective-permute-start | bytes 196616 | tf_op jit(solution)/shard_map/ppermute | solution.py:261
  30.2 5.2 %collective-permute-start.8 = (f16[64,512]{1,0:T(8,128)(2,1)S(1)}, f16[64,512]{1,0:T(8,128)(2,1)S(1)}, u32[]{:S(2)}, u32[]{:S(2)}) collective-permute-start(f16[64,512]{1,0:T(8,128)(2,1)S(1)} %get-tuple-element.29), channel_id=1, source_target_pairs={{0,6},{2,0},{4,2},{6,4},{1,7},{3,1},{5,3},{7,5},{8,14},{10,8},{12,... | collective-permute-start | bytes 196616 | tf_op jit(solution)/shard_map/ppermute | solution.py:261

commit v3 on v1

--- a/solution.py
+++ b/solution.py
@@ -200,26 +200,26 @@
     return call(functools.partial(add_kernel, order_total), shape, [VMEM] * 2, LONG)(total, piece)
 
 
-def last_kernel(order_total, sum_ref, piece_ref, out_ref):
-    share, half = out_ref.shape[0], out_ref.shape[1] // 2
+def last_kernel(order_total, sum_ref, piece_ref, same_ref, cross_ref):
+    share, half = same_ref.shape
     same, cross = factors(piece_ref[:8, :half], share, order_total)
-    sub = lax.axis_index("sub")
-    at = pl.ds(pl.multiple_of(sub * half, half), half)
-    other = pl.ds(pl.multiple_of((1 - sub) * half, half), half)
-    out_ref[:, other] = sum_ref[:, half:] + piece_ref[:, half:] * cross
-    out_ref[:, at] = sum_ref[:, :half] + piece_ref[:, :half] * same
+    cross_ref[...] = sum_ref[:, half:] + piece_ref[:, half:] * cross
+    same_ref[...] = sum_ref[:, :half] + piece_ref[:, :half] * same
     head = sum_ref[:8, :half] + piece_ref[:8, :half] * same
     row = lax.broadcasted_iota(jnp.int32, head.shape, 0)
     col = lax.broadcasted_iota(jnp.int32, head.shape, 1)
     start = col == lax.axis_index("row") * share
     for line in (1, 2):
         head = jnp.where((row == line) & start, pick(head[:1], line, share), head)
-    out_ref[:8, at] = head
+    same_ref[:8, :] = head
 
 
 def last_sum(total, piece, order_total):
-    shape = jax.ShapeDtypeStruct(total.shape, jnp.float32)
-    return call(functools.partial(last_kernel, order_total), shape, [VMEM] * 2)(total, piece)
+    share, columns = total.shape
+    shape = jax.ShapeDtypeStruct((share, columns // 2), jnp.float32)
+    same, cross = call(functools.partial(last_kernel, order_total), (shape, shape), [VMEM] * 2)(total, piece)
+    first = lax.axis_index("sub") == 0
+    return jnp.concatenate([jnp.where(first, same, cross), jnp.where(first, cross, same)], axis=1)
 
 
 def image_kernel(band_ref, sa_ref, sb_ref, out_ref):

time: 36.5 us -> 36.5 us (level)
  other arithmetic: 0.07 us -> 0.75 us
  Pallas kernels: 5.21 us -> 4.56 us
    reshape x0 -> x1, other arithmetic: none -> 0.67 us  [body(): return margin.reshape(1, 1, share, 2 * half)]
    pallas_call x1, Pallas kernels: 0.91 us -> 0.26 us  [last_sum(): call(functools.partial(last_kernel, order_total), (shape, shape), [VMEM]...]
where the time goes in v3:
time: 36.5 us; the launch traced here: 36.4 us
  waiting for transfers between devices  16.5 us (45%)
  starting transfers between devices  11.2 us (31%)
  Pallas kernels  4.56 us (12%)
  between operations  2.27 us (6%)
  local copies, waits for them, and re-layouts  1.1 us (3%)
  other arithmetic  0.75 us (2%)
    ppermute x2, starting transfers between devices, halos_of(): lax.ppermute(low, 'row', backward)  6.92 us
    ppermute x2, waiting for transfers between devices, halos_of(): lax.ppermute(high, 'row', forward)  6.76 us
    ppermute x3, waiting for transfers between devices, send_shares(): arrived.append(lax.ppermute(part, 'row', ring))  4.96 us
    ppermute x3, starting transfers between devices, send_shares(): arrived.append(lax.ppermute(part, 'row', ring))  4.04 us
    ppermute x2, waiting for transfers between devices, halos_of(): lax.ppermute(low, 'row', backward)  3.96 us
    pallas_call x1, Pallas kernels, band_parts(): call(functools.partial(band_kernel, total_blocks), (jax.ShapeDtypeStruct(...  1.52 us
    slice x1, local copies, waits for them, and re-layouts, body(): xa, xb = (x[:wide], x[wide:])  1.05 us
    ppermute x1, waiting for transfers between devices, body(): ob = lax.ppermute(fb, 'sub', swap)  0.84 us
  transfers between devices with their start and end apart: 9, of which 8 were waited for; matrix products, arithmetic and copies ran while one was open for 0% of the time, Pallas kernels for 11%

profile of v3, /device:TPU:0, one launch (start us, length us, event | category | flops | bytes accessed | tf_op | source)
XLA Modules:
  0.0 36.4 jit_solution(7727437370104751349)
XLA Ops:
  0.0 1.0 %slice_bitcast_fusion = (bf16[384,256]{1,0:T(8,128)(2,1)S(1)}, bf16[384,256]{1,0:T(8,128)(2,1)S(1)}) fusion(bf16[1,768,256]{2,1,0:T(8,128)(2,1)} %param.8), kind=kLoop, calls=%fused_computation | loop fusion | bytes 786432 | tf_op jit(solution)/shard_map/slice | solution.py:263
  1.1 5.1 %collective-permute-start.1 = (bf16[384,256]{1,0:T(8,128)(2,1)S(1)}, bf16[384,256]{1,0:T(8,128)(2,1)S(1)}, u32[]{:S(2)}, u32[]{:S(2)}) collective-permute-start(bf16[384,256]{1,0:T(8,128)(2,1)S(1)} %get-tuple-element.32.xa_ref.x_ref), channel_id=1, source_target_pairs={{2,0},{4,2},{6,4},{0,6},{3,1},{5,3},{7,5},{1,7},{10,8},{12,10},{14... | collective-permute-start | bytes 589832 | tf_op jit(solution)/shard_map/ppermute | solution.py:260
  6.2 0.0 copy-start
  6.2 0.0 copy-start.1
  6.2 0.0 collective-permute-start
  7.6 0.0 copy-done
  7.6 0.0 copy-done.1
  7.6 1.5 %shard_map.66 = (bf16[768,1152]{1,0:T(8,128)(2,1)S(1)}, f32[768,256]{1,0:T(8,128)S(1)}) custom-call(f32[8,256]{1,0:T(8,128)S(1)} %shard_map.65.table_ref, s32[6,6]{1,0:T(8,128)S(1)} %copy-done.1, bf16[6,6,128,128]{3,2,1,0:T(8,128)(2,1)S(1)} %copy-done, bf16[384,256]{1,0:T(8,128)(2,1)S(1)} %get-tuple-element.32.xa_ref.x_ref, ...), custom_call_target="tpu_custom_call" | custom-call | flops 1000 | bytes 1000 | tf_op jit(solution)/shard_map/pallas_call | solution.py:86
  9.1 2.3 %collective-permute-done.1.halo_ref = bf16[384,256]{1,0:T(8,128)(2,1)S(1)} collective-permute-done((bf16[384,256]{1,0:T(8,128)(2,1)S(1)}, bf16[384,256]{1,0:T(8,128)(2,1)S(1)}, u32[]{:S(2)}, u32[]{:S(2)}) %collective-permute-start.1) | collective-permute-done | bytes 196640 | tf_op jit(solution)/shard_map/ppermute | solution.py:260
  11.5 0.3 shard_map.67.sb_ref.s_ref
  11.7 0.1 collective-permute-start.2
  11.8 4.2 %collective-permute-done.halo_ref = bf16[384,256]{1,0:T(8,128)(2,1)S(1)} collective-permute-done((bf16[384,256]{1,0:T(8,128)(2,1)S(1)}, bf16[384,256]{1,0:T(8,128)(2,1)S(1)}, u32[]{:S(2)}, u32[]{:S(2)}) %collective-permute-start) | collective-permute-done | bytes 196640 | tf_op jit(solution)/shard_map/ppermute | solution.py:260
  16.0 0.3 shard_map.68.sa_ref.s_ref
  16.2 1.8 %collective-permute-start.3 = (bf16[384,256]{1,0:T(8,128)(2,1)S(1)}, bf16[384,256]{1,0:T(8,128)(2,1)S(1)}, u32[]{:S(2)}, u32[]{:S(2)}) collective-permute-start(bf16[384,256]{1,0:T(8,128)(2,1)S(1)} %shard_map.68.sa_ref.s_ref), channel_id=1, source_target_pairs={{2,0},{4,2},{6,4},{0,6},{3,1},{5,3},{7,5},{1,7},{10,8},{12,10},{14... | collective-permute-start | bytes 589832 | tf_op jit(solution)/shard_map/ppermute | solution.py:260
  18.7 0.6 %shard_map.70.image_ref = f32[768,256]{1,0:T(8,128)S(1)} custom-call(bf16[768,1152]{1,0:T(8,128)(2,1)S(1)} %get-tuple-element.21.band_ref, bf16[384,256]{1,0:T(8,128)(2,1)S(1)} %shard_map.68.sa_ref.s_ref, bf16[384,256]{1,0:T(8,128)(2,1)S(1)} %shard_map.67.sb_ref.s_ref), custom_call_target="tpu_custom_call" | custom-call | flops 1000 | bytes 1000 | tf_op jit(solution)/shard_map/pallas_call | solution.py:232
  19.3 2.6 %collective-permute-done.2.halo_ref = bf16[384,256]{1,0:T(8,128)(2,1)S(1)} collective-permute-done((bf16[384,256]{1,0:T(8,128)(2,1)S(1)}, bf16[384,256]{1,0:T(8,128)(2,1)S(1)}, u32[]{:S(2)}, u32[]{:S(2)}) %collective-permute-start.2) | collective-permute-done | bytes 196640 | tf_op jit(solution)/shard_map/ppermute | solution.py:260
  21.9 0.3 shard_map.71.fa_ref
  22.2 0.1 collective-permute-start.4
  22.2 1.6 %collective-permute-done.3.halo_ref = bf16[384,256]{1,0:T(8,128)(2,1)S(1)} collective-permute-done((bf16[384,256]{1,0:T(8,128)(2,1)S(1)}, bf16[384,256]{1,0:T(8,128)(2,1)S(1)}, u32[]{:S(2)}, u32[]{:S(2)}) %collective-permute-start.3) | collective-permute-done | bytes 196640 | tf_op jit(solution)/shard_map/ppermute | solution.py:260
  23.9 0.3 shard_map.72.fb_ref
  24.1 0.1 collective-permute-start.5
  24.3 0.0 collective-permute-done.4.oa_ref
  24.3 0.5 %shard_map.73 = (f32[256,512]{1,0:T(8,128)S(1)}, bf16[256,384]{1,0:T(8,128)(2,1)S(1)}) custom-call(bf16[384,256]{1,0:T(8,128)(2,1)S(1)} %shard_map.71.fa_ref, bf16[384,256]{1,0:T(8,128)(2,1)S(1)} %shard_map.72.fb_ref, bf16[384,256]{1,0:T(8,128)(2,1)S(1)} %collective-permute-done.4.oa_ref), custom_call_target="tpu_custom_call" | custom-call | flops 1000 | bytes 1000 | tf_op jit(solution)/shard_map/pallas_call | solution.py:150
  24.8 0.8 %collective-permute-done.5.ob_ref = bf16[384,256]{1,0:T(8,128)(2,1)S(1)} collective-permute-done((bf16[384,256]{1,0:T(8,128)(2,1)S(1)}, bf16[384,256]{1,0:T(8,128)(2,1)S(1)}, u32[]{:S(2)}, u32[]{:S(2)}) %collective-permute-start.5) | collective-permute-done | bytes 196640 | tf_op jit(solution)/shard_map/ppermute | solution.py:276
  25.6 0.4 %shard_map.74.coded_ref = f32[256,512]{1,0:T(8,128)S(1)} custom-call(f32[256,512]{1,0:T(8,128)S(1)} %get-tuple-element.25.early_ref, bf16[256,384]{1,0:T(8,128)(2,1)S(1)} %get-tuple-element.26.turned_ref, bf16[384,256]{1,0:T(8,128)(2,1)S(1)} %collective-permute-done.5.ob_ref), custom_call_target="tpu_custom_call" | custom-call | flops 1000 | bytes 1000 | tf_op jit(solution)/shard_map/pallas_call | solution.py:163
  26.1 1.1 %collective-permute-start.6 = (f16[64,512]{1,0:T(8,128)(2,1)S(1)}, f16[64,512]{1,0:T(8,128)(2,1)S(1)}, u32[]{:S(2)}, u32[]{:S(2)}) collective-permute-start(f16[64,512]{1,0:T(8,128)(2,1)S(1)} %get-tuple-element.35), channel_id=1, source_target_pairs={{0,2},{2,4},{4,6},{6,0},{1,3},{3,5},{5,7},{7,1},{8,10},{10,12},{12... | collective-permute-start | bytes 196616 | tf_op jit(solution)/shard_map/ppermute | solution.py:241
  27.2 2.9 %collective-permute-start.7 = (f16[64,512]{1,0:T(8,128)(2,1)S(1)}, f16[64,512]{1,0:T(8,128)(2,1)S(1)}, u32[]{:S(2)}, u32[]{:S(2)}) collective-permute-start(f16[64,512]{1,0:T(8,128)(2,1)S(1)} %get-tuple-element.34), channel_id=1, source_target_pairs={{0,4},{2,6},{4,0},{6,2},{1,5},{3,7},{5,1},{7,3},{8,12},{10,14},{12... | collective-permute-start | bytes 196616 | tf_op jit(solution)/shard_map/ppermute | solution.py:241
  30.2 0.0 collective-permute-start.8
  30.2 2.9 %collective-permute-done.6 = f16[64,512]{1,0:T(8,128)(2,1)S(1)} collective-permute-done((f16[64,512]{1,0:T(8,128)(2,1)S(1)}, f16[64,512]{1,0:T(8,128)(2,1)S(1)}, u32[]{:S(2)}, u32[]{:S(2)}) %collective-permute-start.6) | collective-permute-done | bytes 65568 | tf_op jit(solution)/shard_map/ppermute | solution.py:241
  33.1 0.1 shard_map.75.sum_ref
  33.2 1.8 %collective-permute-done.7 = f16[64,512]{1,0:T(8,128)(2,1)S(1)} collective-permute-done((f16[64,512]{1,0:T(8,128)(2,1)S(1)}, f16[64,512]{1,0:T(8,128)(2,1)S(1)}, u32[]{:S(2)}, u32[]{:S(2)}) %collective-permute-start.7) | collective-permute-done | bytes 65568 | tf_op jit(solution)/shard_map/ppermute | solution.py:241
  35.0 0.1 shard_map.76.sum_ref
  35.1 0.3 collective-permute-done.8
  35.4 0.3 shard_map.77
  35.7 0.7 %maximum_bitcast_fusion = f32[1,1,64,512]{3,2,1,0:T(8,128)} fusion(f32[64,256]{1,0:T(8,128)S(1)} %get-tuple-element.37, f32[64,256]{1,0:T(8,128)S(1)} %get-tuple-element.36), kind=kLoop, calls=%fused_computation.2 | loop fusion | flops 32768 | bytes 262144 | tf_op jit(solution)/shard_map/reshape | solution.py:285
  (9 shorter events, 0.1 us)
Async XLA Ops:
  1.1 10.4 %collective-permute-start.1 = (bf16[384,256]{1,0:T(8,128)(2,1)S(1)}, bf16[384,256]{1,0:T(8,128)(2,1)S(1)}, u32[]{:S(2)}, u32[]{:S(2)}) collective-permute-start(bf16[384,256]{1,0:T(8,128)(2,1)S(1)} %get-tuple-element.32.xa_ref.x_ref), channel_id=1, source_target_pairs={{2,0},{4,2},{6,4},{0,6},{3,1},{5,3},{7,5},{1,7},{10,8},{12,10},{14... | collective-permute-start | bytes 589832 | tf_op jit(solution)/shard_map/ppermute | solution.py:260
  6.2 1.4 %copy-start = (bf16[6,6,128,128]{3,2,1,0:T(8,128)(2,1)S(1)}, bf16[6,6,128,128]{3,2,1,0:T(8,128)(2,1)}, u32[]{:S(2)}) copy-start(bf16[6,6,128,128]{3,2,1,0:T(8,128)(2,1)} %hop_ref.1) | copy-start | bytes 3538948
  6.2 1.4 %copy-start.1 = (s32[6,6]{1,0:T(8,128)S(1)}, s32[6,6]{1,0:T(8,128)}, u32[]{:S(2)}) copy-start(s32[6,6]{1,0:T(8,128)} %pattern_ref.1) | copy-start | bytes 436
  6.2 9.8 %collective-permute-start = (bf16[384,256]{1,0:T(8,128)(2,1)S(1)}, bf16[384,256]{1,0:T(8,128)(2,1)S(1)}, u32[]{:S(2)}, u32[]{:S(2)}) collective-permute-start(bf16[384,256]{1,0:T(8,128)(2,1)S(1)} %get-tuple-element.31.xb_ref.x_ref), channel_id=1, source_target_pairs={{0,2},{2,4},{4,6},{6,0},{1,3},{3,5},{5,7},{7,1},{8,10},{10,12},{12... | collective-permute-start | bytes 589832 | tf_op jit(solution)/shard_map/ppermute | solution.py:260
  11.7 10.1 %collective-permute-start.2 = (bf16[384,256]{1,0:T(8,128)(2,1)S(1)}, bf16[384,256]{1,0:T(8,128)(2,1)S(1)}, u32[]{:S(2)}, u32[]{:S(2)}) collective-permute-start(bf16[384,256]{1,0:T(8,128)(2,1)S(1)} %shard_map.67.sb_ref.s_ref), channel_id=1, source_target_pairs={{0,2},{2,4},{4,6},{6,0},{1,3},{3,5},{5,7},{7,1},{8,10},{10,12},{12... | collective-permute-start | bytes 589832 | tf_op jit(solution)/shard_map/ppermute | solution.py:260
  16.2 7.6 %collective-permute-start.3 = (bf16[384,256]{1,0:T(8,128)(2,1)S(1)}, bf16[384,256]{1,0:T(8,128)(2,1)S(1)}, u32[]{:S(2)}, u32[]{:S(2)}) collective-permute-start(bf16[384,256]{1,0:T(8,128)(2,1)S(1)} %shard_map.68.sa_ref.s_ref), channel_id=1, source_target_pairs={{2,0},{4,2},{6,4},{0,6},{3,1},{5,3},{7,5},{1,7},{10,8},{12,10},{14... | collective-permute-start | bytes 589832 | tf_op jit(solution)/shard_map/ppermute | solution.py:260
  22.2 2.1 %collective-permute-start.4 = (bf16[384,256]{1,0:T(8,128)(2,1)S(1)}, bf16[384,256]{1,0:T(8,128)(2,1)S(1)}, u32[]{:S(2)}, u32[]{:S(2)}) collective-permute-start(bf16[384,256]{1,0:T(8,128)(2,1)S(1)} %shard_map.71.fa_ref), channel_id=1, source_target_pairs={{0,1},{1,0},{2,3},{3,2},{4,5},{5,4},{6,7},{7,6},{8,9},{9,8},{10,11... | collective-permute-start | bytes 589832 | tf_op jit(solution)/shard_map/ppermute | solution.py:274
  24.1 1.5 %collective-permute-start.5 = (bf16[384,256]{1,0:T(8,128)(2,1)S(1)}, bf16[384,256]{1,0:T(8,128)(2,1)S(1)}, u32[]{:S(2)}, u32[]{:S(2)}) collective-permute-start(bf16[384,256]{1,0:T(8,128)(2,1)S(1)} %shard_map.72.fb_ref), channel_id=1, source_target_pairs={{0,1},{1,0},{2,3},{3,2},{4,5},{5,4},{6,7},{7,6},{8,9},{9,8},{10,11... | collective-permute-start | bytes 589832 | tf_op jit(solution)/shard_map/ppermute | solution.py:276
  26.1 6.9 %collective-permute-start.6 = (f16[64,512]{1,0:T(8,128)(2,1)S(1)}, f16[64,512]{1,0:T(8,128)(2,1)S(1)}, u32[]{:S(2)}, u32[]{:S(2)}) collective-permute-start(f16[64,512]{1,0:T(8,128)(2,1)S(1)} %get-tuple-element.35), channel_id=1, source_target_pairs={{0,2},{2,4},{4,6},{6,0},{1,3},{3,5},{5,7},{7,1},{8,10},{10,12},{12... | collective-permute-start | bytes 196616 | tf_op jit(solution)/shard_map/ppermute | solution.py:241
  27.2 7.8 %collective-permute-start.7 = (f16[64,512]{1,0:T(8,128)(2,1)S(1)}, f16[64,512]{1,0:T(8,128)(2,1)S(1)}, u32[]{:S(2)}, u32[]{:S(2)}) collective-permute-start(f16[64,512]{1,0:T(8,128)(2,1)S(1)} %get-tuple-element.34), channel_id=1, source_target_pairs={{0,4},{2,6},{4,0},{6,2},{1,5},{3,7},{5,1},{7,3},{8,12},{10,14},{12... | collective-permute-start | bytes 196616 | tf_op jit(solution)/shard_map/ppermute | solution.py:241
  30.2 5.2 %collective-permute-start.8 = (f16[64,512]{1,0:T(8,128)(2,1)S(1)}, f16[64,512]{1,0:T(8,128)(2,1)S(1)}, u32[]{:S(2)}, u32[]{:S(2)}) collective-permute-start(f16[64,512]{1,0:T(8,128)(2,1)S(1)} %get-tuple-element.33), channel_id=1, source_target_pairs={{0,6},{2,0},{4,2},{6,4},{1,7},{3,1},{5,3},{7,5},{8,14},{10,8},{12,... | collective-permute-start | bytes 196616 | tf_op jit(solution)/shard_map/ppermute | solution.py:241
